TPU v7x, 32 devices: a whole 2x2x4 slice. The times are simulated.
32 devices in a mesh: shots: 2 (over x), lat: 16 (over z, y, core).
Axes of the slice: x: 2, y: 2, z: 4, core: 2. Of those that a mesh axis runs over, the one named last changes fastest.
Arguments:
- source_field: float32 [4, 2, 1024, 1024], P('shots', None, 'lat'), parts along dimension 0, may hold values from -6 to 6
- receiver_field: float32 [4, 2, 1024, 1024], P('shots', None, 'lat'), parts along dimension 0, may hold values from -6 to 6
- ref_slowness: float32 [2], replicated, may hold values from 0.6 to 1.3
- omega: float32 [2], replicated, may hold values from 1 to 2.5
- interp_index: int32 [1024, 1024], P('lat'), may hold values from 0 to 7
- lags: int32 [16], replicated, may hold values from -16 to 16, as said below
Outputs:
- images: float32 [32, 1024, 1024], P('shots', 'lat'), parts along dimension 0
There are 2 independent parts, one for each index of `shots`. A program takes and returns all parts, laid end to end along the dimension named above; an argument that names none is the same for every part. Nothing has to cross between parts.
Inputs may be any that keep to these rules, and one draw needn't show every extreme that they name: `lags`: offsets lie in -16 to 16, and both ends occur.
All inputs are finite; a program needn't handle non-finite values.
Results may differ from a plain program's by a relative error of at most 0.0003.
Values sent between devices are 32-bit elements; how exact they have to be, the bound alone decides.
A program may use at most 128 MiB of HBM per device.

v0:
```python
import functools
import math

import jax
import jax.numpy as jnp
import ml_dtypes
import numpy as np
from jax import lax
from jax.experimental import pallas as pl
from jax.experimental.pallas import tpu as pltpu
from jax.sharding import PartitionSpec as P

HMAX = 16
INTERP = 8


depth_step = 2.0
highest = lax.Precision.HIGHEST


def extended(block, sides, width):
    for axis, dim in sides:
        count = lax.axis_size(axis)
        forward = [(i, i + 1) for i in range(count - 1)]
        backward = [(target, source) for source, target in forward]
        low = lax.ppermute(
            lax.slice_in_dim(block, block.shape[dim] - width, None, axis=dim), axis, forward
        )
        high = lax.ppermute(lax.slice_in_dim(block, 0, width, axis=dim), axis, backward)
        block = jnp.concatenate([low, block, high], axis=dim)
    return block


def dft_tables(count):
    index = jnp.arange(count, dtype=jnp.int32)
    turns = index[:, None] * index[None, :] % count
    angle = turns.astype(jnp.float32) * (2.0 * math.pi / count)
    return (jnp.cos(angle), jnp.sin(angle))


def wave_numbers(count):
    index = jnp.arange(count, dtype=jnp.int32)
    signed = jnp.where(index < count // 2, index, index - count)
    return signed.astype(jnp.float32) * (2.0 * math.pi / count)


def factor_pair(count):
    first = 1
    for divisor in range(1, int(math.isqrt(count)) + 1):
        if count % divisor == 0:
            first = divisor
    return (first, count // first)


def complex_apply(real_part, imag_part, cosine, sine, form, sign):
    stacked = jnp.stack([real_part, imag_part], axis=0)
    with_cos = jnp.einsum(form, stacked, cosine, precision=highest)
    with_sin = jnp.einsum(form, stacked, sine, precision=highest)
    return (with_cos[0] - sign * with_sin[1], with_cos[1] + sign * with_sin[0])


def dft_axis(real_part, imag_part, axis, sign, factor):
    count = real_part.shape[axis]
    first, second = factor_pair(count)
    real_part = jnp.moveaxis(real_part, axis, -1)
    imag_part = jnp.moveaxis(imag_part, axis, -1)
    leading = real_part.shape[:-1]
    real_part = real_part.reshape(leading + (first, second))
    imag_part = imag_part.reshape(leading + (first, second))
    cos_a, sin_a = dft_tables(first)
    real_part, imag_part = complex_apply(
        real_part, imag_part, cos_a, sin_a, "...ab,ac->...cb", sign
    )
    row_index = jnp.arange(first, dtype=jnp.int32)[:, None]
    col_index = jnp.arange(second, dtype=jnp.int32)[None, :]
    twist = (row_index * col_index % count).astype(jnp.float32) * (2.0 * math.pi / count)
    cos_t = jnp.cos(twist)
    sin_t = sign * jnp.sin(twist)
    real_part, imag_part = (
        real_part * cos_t - imag_part * sin_t,
        real_part * sin_t + imag_part * cos_t,
    )
    cos_b, sin_b = dft_tables(second)
    real_part, imag_part = complex_apply(
        real_part, imag_part, cos_b, sin_b, "...cb,bd->...cd", sign
    )
    real_part = jnp.swapaxes(real_part, -1, -2).reshape(leading + (count,)) * factor
    imag_part = jnp.swapaxes(imag_part, -1, -2).reshape(leading + (count,)) * factor
    return (jnp.moveaxis(real_part, -1, axis), jnp.moveaxis(imag_part, -1, axis))


def send_out_each(spectrum):
    return lax.all_to_all(spectrum, "lat", split_axis=4, concat_axis=3, tiled=True)


def send_back_each(fields):
    return lax.all_to_all(fields, "lat", split_axis=4, concat_axis=5, tiled=True)


def propagate(fields, omegas, ref_slowness, send_out, send_back):
    n_y = fields.shape[4]
    n_x = fields.shape[3] * lax.axis_size("lat")
    real_part, imag_part = dft_axis(fields[:, :, 0], fields[:, :, 1], 3, -1.0, 1.0)
    turned = send_out(jnp.stack([real_part, imag_part], axis=2))
    n_cols = turned.shape[4]
    real_part, imag_part = dft_axis(turned[:, :, 0], turned[:, :, 1], 2, -1.0, 1.0)
    real_part = jnp.swapaxes(real_part, 2, 3)
    imag_part = jnp.swapaxes(imag_part, 2, 3)
    ky_all = wave_numbers(n_y)
    ky = lax.dynamic_slice_in_dim(ky_all, lax.axis_index("lat") * n_cols, n_cols)
    kx = wave_numbers(n_x)
    lateral = ky[:, None] ** 2 + kx[None, :] ** 2
    direction = jnp.array([-1.0, 1.0], dtype=jnp.float32)[:, None, None, None]
    shifted = []
    for j in range(2):
        vertical = (omegas * ref_slowness[j]) ** 2
        arg = vertical[:, None, None] - lateral[None]
        phase = jnp.sqrt(jnp.maximum(arg, 0.0)) * depth_step
        decay = jnp.exp(-jnp.sqrt(jnp.maximum(-arg, 0.0)) * depth_step)
        cos_shift = (decay * jnp.cos(phase))[None]
        sin_shift = direction * (decay * jnp.sin(phase))[None]
        new_real = real_part * cos_shift - imag_part * sin_shift
        new_imag = real_part * sin_shift + imag_part * cos_shift
        back_real, back_imag = dft_axis(new_real, new_imag, 3, 1.0, 1.0 / n_x)
        back_real = jnp.swapaxes(back_real, 2, 3)
        back_imag = jnp.swapaxes(back_imag, 2, 3)
        shifted.append(jnp.stack([back_real, back_imag], axis=2))
    returned = send_back(jnp.stack(shifted, axis=0))
    out_real, out_imag = dft_axis(returned[:, :, :, 0], returned[:, :, :, 1], 4, 1.0, 1.0 / n_y)
    return jnp.stack([out_real, out_imag], axis=3)


def local(source_field, receiver_field, ref_slowness, omega, interp_index, lags):
    fields = jnp.stack([source_field, receiver_field], axis=0)
    pieces = []
    for step in range(fields.shape[1]):
        pieces.append(
            propagate(
                fields[:, step : step + 1],
                omega[step : step + 1],
                ref_slowness,
                send_out_each,
                send_back_each,
            )
        )
    references = jnp.concatenate(pieces, axis=2)
    weight = interp_index.astype(jnp.float32) / (INTERP - 1)
    migrated = (1.0 - weight) * references[0] + weight * references[1]
    padded = extended(migrated, (("lat", 3),), HMAX)
    rows = migrated.shape[3]

    def one_offset(lag):
        source_rows = lax.dynamic_slice_in_dim(padded[0], HMAX - lag, rows, 2)
        receiver_rows = lax.dynamic_slice_in_dim(padded[1], HMAX + lag, rows, 2)
        return jnp.sum(source_rows * receiver_rows, axis=(0, 1))

    return lax.map(one_offset, lags)


RADIX = 4
SUB = 256
POINTS = RADIX * SUB
PEERS = 16
ROWS = POINTS // PEERS
LANES = 2 * ROWS
BANDS = POINTS // LANES
MESH = pl.DeviceIdType.MESH


def fourier_tables():
    r = np.arange(RADIX)[:, None, None]
    m = np.arange(SUB)[None, :, None]
    y = np.arange(SUB)[None, None, :]
    angle = ((r + RADIX * m) * y % POINTS) * (2.0 * np.pi / POINTS)
    both = np.stack([np.cos(angle), np.sin(angle)], axis=1).astype(np.float32)
    high = both.astype(ml_dtypes.bfloat16)
    low = (both - high.astype(np.float32)).astype(ml_dtypes.bfloat16)
    straight = np.stack([high, low], axis=2)
    return np.stack([straight, np.swapaxes(straight, -1, -2)])


def split(value):
    high = value.astype(jnp.bfloat16)
    low = (value - high.astype(jnp.float32)).astype(jnp.bfloat16)
    return high, low


def dot(a, b):
    return jnp.dot(a, b, preferred_element_type=jnp.float32)


def table_left(tab_ref, turned, r, trig, pair):
    high, low = tab_ref[turned, r, trig, 0], tab_ref[turned, r, trig, 1]
    return dot(high, pair[0]) + (dot(high, pair[1]) + dot(low, pair[0]))


def table_right(tab_ref, turned, r, trig, pair):
    high, low = tab_ref[turned, r, trig, 0], tab_ref[turned, r, trig, 1]
    return dot(pair[0], high) + (dot(pair[1], high) + dot(pair[0], low))


def forward_four(re, im):
    pr, mr, qr, nr = re[0] + re[2], re[0] - re[2], re[1] + re[3], re[1] - re[3]
    pi, mi, qi, ni = im[0] + im[2], im[0] - im[2], im[1] + im[3], im[1] - im[3]
    return (
        [pr + qr, mr + ni, pr - qr, mr - ni],
        [pi + qi, mi - nr, pi - qi, mi + nr],
    )


def backward_four(re, im):
    pr, mr, qr, nr = re[0] + re[2], re[0] - re[2], re[1] + re[3], re[1] - re[3]
    pi, mi, qi, ni = im[0] + im[2], im[0] - im[2], im[1] + im[3], im[1] - im[3]
    return (
        [pr + qr, mr - ni, pr - qr, mr + ni],
        [pi + qi, mi + nr, pi - qi, mi - nr],
    )


def signed_wave(index):
    signed = jnp.where(index < POINTS // 2, index, index - POINTS)
    return signed.astype(jnp.float32) * (2.0 * math.pi / POINTS)


def series(square, terms):
    total = jnp.full_like(square, terms[-1])
    for term in terms[-2::-1]:
        total = total * square + term
    return total


SIN_TERMS = [(-1.0) ** i / math.factorial(2 * i + 1) for i in range(8)]
COS_TERMS = [(-1.0) ** i / math.factorial(2 * i) for i in range(8)]


def shift_pair(arg):
    root = jnp.sqrt(jnp.abs(arg))
    half = root - 0.5 * math.pi
    square = half * half
    sine = half * series(square, SIN_TERMS)
    cosine = series(square, COS_TERMS)
    moving = arg > 0.0
    decay = jnp.exp(-depth_step * root)
    real = jnp.where(moving, 2.0 * sine * sine - 1.0, decay)
    imag = jnp.where(moving, -2.0 * sine * cosine, 0.0)
    return real, imag


def halves(first, second, low_half):
    low = jnp.where(low_half, first, pltpu.roll(second, ROWS, 1))
    high = jnp.where(low_half, pltpu.roll(first, ROWS, 1), second)
    return low, high


def migrate_kernel(
    omega_ref, slow_ref, src_ref, rec_ref, index_ref, tab_ref, out_ref,
    send_f, recv_f, send_b, recv_b, spec, shift, first_ref,
    sem_fs, sem_fr, sem_bs, sem_br, sem_hs, sem_hr,
):
    me = lax.axis_index("lat")
    n = PEERS
    lane = lax.broadcasted_iota(jnp.int32, (ROWS, LANES), 1)
    low_half = lane < ROWS

    def copy_f(w, d):
        to = lax.rem(me + d, n)
        return pltpu.make_async_remote_copy(
            src_ref=send_f.at[w, to], dst_ref=recv_f.at[w, me],
            send_sem=sem_fs.at[w, d], recv_sem=sem_fr.at[w, d],
            device_id={"lat": to}, device_id_type=MESH,
        )

    def copy_b(w, j, d):
        to = lax.rem(me + d, n)
        return pltpu.make_async_remote_copy(
            src_ref=send_b.at[w, j, to], dst_ref=recv_b.at[w, j, me],
            send_sem=sem_bs.at[w, j, d], recv_sem=sem_br.at[w, j, d],
            device_id={"lat": to}, device_id_type=MESH,
        )

    def got_f(w, d):
        origin = lax.rem(me + n - d, n)
        return pltpu.make_async_remote_copy(
            src_ref=send_f.at[w, me], dst_ref=recv_f.at[w, origin],
            send_sem=sem_fs.at[w, d], recv_sem=sem_fr.at[w, d],
            device_id={"lat": origin}, device_id_type=MESH,
        )

    def got_b(w, j, d):
        origin = lax.rem(me + n - d, n)
        return pltpu.make_async_remote_copy(
            src_ref=send_b.at[w, j, me], dst_ref=recv_b.at[w, j, origin],
            send_sem=sem_bs.at[w, j, d], recv_sem=sem_br.at[w, j, d],
            device_id={"lat": origin}, device_id_type=MESH,
        )

    def halo(w, side):
        to, take, put = (me + 1, ROWS, 0) if side == 0 else (me - 1, HMAX, HMAX + ROWS)
        return pltpu.make_async_remote_copy(
            src_ref=out_ref.at[w, :, :, :, pl.ds(take, HMAX), :],
            dst_ref=out_ref.at[w, :, :, :, pl.ds(put, HMAX), :],
            send_sem=sem_hs.at[w, side], recv_sem=sem_hr.at[w, side],
            device_id={"lat": to}, device_id_type=MESH,
        )

    def every(body):
        @pl.loop(1, n)
        def _(d):
            body(d)

    barrier = pltpu.get_barrier_semaphore()

    def greet(d):
        pl.semaphore_signal(
            barrier, inc=1, device_id={"lat": lax.rem(me + d, n)}, device_id_type=MESH
        )

    every(greet)

    def rows_forward(w):
        re, im = [], []
        for q in range(RADIX):
            cut = pl.ds(q * SUB, SUB)
            re.append(jnp.concatenate([src_ref[w, 0, :, cut], rec_ref[w, 0, :, cut]], axis=0))
            im.append(jnp.concatenate([src_ref[w, 1, :, cut], rec_ref[w, 1, :, cut]], axis=0))
        re, im = forward_four(re, im)
        for r in range(RADIX):
            pair = split(jnp.concatenate([re[r], im[r]], axis=0))
            with_cos = table_right(tab_ref, 1, r, 0, pair)
            with_sin = table_right(tab_ref, 1, r, 1, pair)
            parts = (
                with_cos[:LANES] + with_sin[LANES:],
                with_cos[LANES:] - with_sin[:LANES],
            )
            for c in range(2):
                for b in range(2):
                    piece = parts[c][:, b * LANES : (b + 1) * LANES]
                    low, high = halves(piece[:ROWS], piece[ROWS:], low_half)
                    peer = RADIX * r + 2 * b
                    send_f[w, peer, c] = low
                    send_f[w, peer + 1, c] = high

    def make_shift(w, j):
        speed = omega_ref[w] * slow_ref[j]
        vertical = speed * speed
        wide = lax.broadcasted_iota(jnp.int32, (ROWS, LANES), 1)
        tall = lax.broadcasted_iota(jnp.int32, (ROWS, LANES), 0)
        place = ROWS * me + lax.rem(wide, ROWS)
        ky = signed_wave(place // SUB + RADIX * lax.rem(place, SUB))
        ky2 = ky * ky
        sign = jnp.where(wide < ROWS, -1.0, 1.0)
        scale = 1.0 / (POINTS * POINTS)

        @pl.loop(0, PEERS)
        def _(block):
            at = ROWS * block
            r = at // SUB
            kx = signed_wave(r + RADIX * (lax.rem(at, SUB) + tall))
            real, imag = shift_pair(vertical - (kx * kx + ky2))
            rows = pl.ds(pl.multiple_of(ROWS * block, ROWS), ROWS)
            shift[w, j, 0, rows, :] = real * scale
            shift[w, j, 1, rows, :] = imag * (sign * scale)

    def columns_forward(w):
        re, im = [], []
        for q in range(RADIX):
            re.append(recv_f[w, 4 * q : 4 * q + 4, 0].reshape(SUB, LANES))
            im.append(recv_f[w, 4 * q : 4 * q + 4, 1].reshape(SUB, LANES))
        re, im = forward_four(re, im)
        for r in range(RADIX):
            pair = split(jnp.concatenate([re[r], im[r]], axis=1))
            with_cos = table_left(tab_ref, 0, r, 0, pair)
            with_sin = table_left(tab_ref, 0, r, 1, pair)
            spec[r, 0] = with_cos[:, :LANES] + with_sin[:, LANES:]
            spec[r, 1] = with_cos[:, LANES:] - with_sin[:, :LANES]

    def columns_backward(w, j):
        re, im = [], []
        for r in range(RADIX):
            cos_shift = shift[w, j, 0, pl.ds(r * SUB, SUB), :]
            sin_shift = shift[w, j, 1, pl.ds(r * SUB, SUB), :]
            new_re = spec[r, 0] * cos_shift - spec[r, 1] * sin_shift
            new_im = spec[r, 0] * sin_shift + spec[r, 1] * cos_shift
            pair = split(jnp.concatenate([new_re, new_im], axis=1))
            with_cos = table_left(tab_ref, 1, r, 0, pair)
            with_sin = table_left(tab_ref, 1, r, 1, pair)
            re.append(with_cos[:, :LANES] - with_sin[:, LANES:])
            im.append(with_cos[:, LANES:] + with_sin[:, :LANES])
        re, im = backward_four(re, im)
        for q in range(RADIX):
            send_b[w, j, 4 * q : 4 * q + 4, 0] = re[q].reshape(4, ROWS, LANES)
            send_b[w, j, 4 * q : 4 * q + 4, 1] = im[q].reshape(4, ROWS, LANES)

    def rows_backward(w, j):
        re, im = [], []
        for r in range(RADIX):
            stacked = []
            for c in range(2):
                sides = [
                    halves(recv_b[w, j, 4 * r + 2 * b, c], recv_b[w, j, 4 * r + 2 * b + 1, c], low_half)
                    for b in range(2)
                ]
                for field in range(2):
                    stacked.append(jnp.concatenate([sides[0][field], sides[1][field]], axis=1))
            pair = split(jnp.concatenate(stacked, axis=0))
            with_cos = table_right(tab_ref, 0, r, 0, pair)
            with_sin = table_right(tab_ref, 0, r, 1, pair)
            re.append(with_cos[:LANES] - with_sin[LANES:])
            im.append(with_cos[LANES:] + with_sin[:LANES])
        parts = backward_four(re, im)
        for q in range(RADIX):
            cut = pl.ds(q * SUB, SUB)
            weight = index_ref[:, cut].astype(jnp.float32) / (INTERP - 1)
            for c in range(2):
                for field in range(2):
                    value = parts[c][q][ROWS * field : ROWS * (field + 1)]
                    if j == 0:
                        first_ref[field, c, :, cut] = (1.0 - weight) * value
                    else:
                        mixed = first_ref[field, c, :, cut] + weight * value
                        for b in range(2):
                            out_ref[w, field, c, 2 * q + b, pl.ds(HMAX, ROWS), :] = (
                                mixed[:, b * LANES : (b + 1) * LANES]
                            )

    @pl.when(me == 0)
    def _():
        for w in range(2):
            out_ref[w, :, :, :, pl.ds(0, HMAX), :] = jnp.zeros((2, 2, BANDS, HMAX, LANES), jnp.float32)

    @pl.when(me == n - 1)
    def _():
        for w in range(2):
            out_ref[w, :, :, :, pl.ds(HMAX + ROWS, HMAX), :] = jnp.zeros((2, 2, BANDS, HMAX, LANES), jnp.float32)

    rows_forward(0)
    pl.semaphore_wait(barrier, n - 1)
    every(lambda d: copy_f(0, d).start())
    rows_forward(1)
    every(lambda d: copy_f(1, d).start())
    for w in range(2):
        recv_f[w, me] = send_f[w, me]
        for j in range(2):
            make_shift(w, j)
    for w in range(2):
        every(lambda d: got_f(w, d).wait_recv())
        columns_forward(w)
        for j in range(2):
            columns_backward(w, j)
            every(lambda d: copy_b(w, j, d).start())
            recv_b[w, j, me] = send_b[w, j, me]
    for w in range(2):
        for j in range(2):
            every(lambda d: got_b(w, j, d).wait_recv())
            rows_backward(w, j)

        @pl.when(me < n - 1)
        def _():
            halo(w, 0).start()

        @pl.when(me > 0)
        def _():
            halo(w, 1).start()

    for w in range(2):
        every(lambda d: copy_f(w, d).wait_send())
        for j in range(2):
            every(lambda d: copy_b(w, j, d).wait_send())

        @pl.when(me < n - 1)
        def _():
            halo(w, 0).wait_send()
            halo(w, 1).wait_recv()

        @pl.when(me > 0)
        def _():
            halo(w, 1).wait_send()
            halo(w, 0).wait_recv()


def image_kernel(lags_ref, fields_ref, out_ref):
    lag = lags_ref[pl.program_id(0)]
    for band in range(BANDS):
        total = None
        for w in range(2):
            for c in range(2):
                source = fields_ref[w, 0, c, band, pl.ds(HMAX - lag, ROWS), :]
                receiver = fields_ref[w, 1, c, band, pl.ds(HMAX + lag, ROWS), :]
                term = source * receiver
                total = term if total is None else total + term
        out_ref[0, :, pl.ds(band * LANES, LANES)] = total


def fused(source_field, receiver_field, ref_slowness, omega, interp_index, lags):
    tables = jnp.asarray(fourier_tables())
    vmem = pl.BlockSpec(memory_space=pltpu.VMEM)
    smem = pl.BlockSpec(memory_space=pltpu.SMEM)
    f32 = jnp.float32
    block = (PEERS, 2, ROWS, LANES)
    dma = pltpu.SemaphoreType.DMA
    migrated = pl.pallas_call(
        migrate_kernel,
        out_shape=jax.ShapeDtypeStruct((2, 2, 2, BANDS, ROWS + 2 * HMAX, LANES), f32),
        in_specs=[smem, smem, vmem, vmem, vmem, vmem],
        out_specs=vmem,
        scratch_shapes=[
            pltpu.VMEM((2,) + block, f32),
            pltpu.VMEM((2,) + block, f32),
            pltpu.VMEM((2, 2) + block, f32),
            pltpu.VMEM((2, 2) + block, f32),
            pltpu.VMEM((RADIX, 2, SUB, LANES), f32),
            pltpu.VMEM((2, 2, 2, POINTS, LANES), f32),
            pltpu.VMEM((2, 2, ROWS, POINTS), f32),
            dma((2, PEERS)), dma((2, PEERS)),
            dma((2, 2, PEERS)), dma((2, 2, PEERS)),
            dma((2, 2)), dma((2, 2)),
        ],
        compiler_params=pltpu.CompilerParams(
            collective_id=0, has_side_effects=True, vmem_limit_bytes=56 * 2**20
        ),
    )(omega, ref_slowness, source_field, receiver_field, interp_index, tables)
    count = lags.shape[0]
    return pl.pallas_call(
        image_kernel,
        grid_spec=pltpu.PrefetchScalarGridSpec(
            num_scalar_prefetch=1,
            grid=(count,),
            in_specs=[pl.BlockSpec(migrated.shape, lambda i, lags: (0,) * 6)],
            out_specs=pl.BlockSpec((1, ROWS, POINTS), lambda i, lags: (i, 0, 0)),
        ),
        out_shape=jax.ShapeDtypeStruct((count, ROWS, POINTS), f32),
        compiler_params=pltpu.CompilerParams(vmem_limit_bytes=32 * 2**20),
    )(lags, migrated)


def body(source_field, receiver_field, ref_slowness, omega, interp_index, lags):
    args = (source_field, receiver_field, ref_slowness, omega, interp_index, lags)
    fits = source_field.shape == (2, 2, ROWS, POINTS) and lax.axis_size("lat") == PEERS
    return fused(*args) if fits else local(*args)


def solution(mesh):
    in_specs = (
        P("shots", None, "lat", None),
        P("shots", None, "lat", None),
        P(),
        P(),
        P("lat", None),
        P(),
    )
    out_specs = P("shots", "lat", None)
    return jax.shard_map(body, mesh=mesh, in_specs=in_specs, out_specs=out_specs, check_vma=False)
```

profile of v0, /device:TPU:12, one launch (start us, length us, event | category | flops | bytes accessed | tf_op | source)
XLA Modules:
  0.0 164.6 jit_solution(15015703883621300068)
XLA Ops:
  0.0 0.0 copy-start.1
  0.0 155.1 %shard_map.73.fields_ref = f32[2,2,2,8,96,128]{5,4,3,2,1,0:T(8,128)} custom-call(f32[2]{0:T(128)} %omega_ref.1, f32[2]{0:T(128)} %slow_ref.1, f32[2,2,64,1024]{3,2,1,0:T(8,128)} %src_ref.1, f32[2,2,64,1024]{3,2,1,0:T(8,128)} %rec_ref.1, s32[64,1024]{1,0:T(8,128)} %index_ref.1, bf16[2,4,2,2,256,256]{5,4,3,2,1,0:T(8,128)(2,1)} %constant.2.clone.tab_ref), custom_call_target="tpu_custom_call" | custom-call | tf_op jit(solution)/shard_map/pallas_call | solution.py:501
  155.1 0.0 copy-done.1
  155.1 0.0 copy-start
  155.1 1.9 %copy-done = f32[2,2,2,8,96,128]{5,4,3,2,1,0:T(8,128)S(1)} copy-done((f32[2,2,2,8,96,128]{5,4,3,2,1,0:T(8,128)S(1)}, f32[2,2,2,8,96,128]{5,4,3,2,1,0:T(8,128)}, u32[]{:S(2)}) %copy-start) | copy-done | bytes 3145752
  157.0 7.6 %shard_map.74 = f32[16,64,1024]{2,1,0:T(8,128)} custom-call(s32[16]{0:T(128)S(1)} %copy-done.1, f32[2,2,2,8,96,128]{5,4,3,2,1,0:T(8,128)S(1)} %copy-done), custom_call_target="tpu_custom_call" | custom-call | tf_op jit(solution)/shard_map/pallas_call | solution.py:523
Async XLA Ops:
  0.0 155.1 %copy-start.1 = (s32[16]{0:T(128)S(1)}, s32[16]{0:T(128)}, u32[]{:S(2)}) copy-start(s32[16]{0:T(128)} %lags_ref.1) | copy-start | bytes 196
  155.1 1.9 %copy-start = (f32[2,2,2,8,96,128]{5,4,3,2,1,0:T(8,128)S(1)}, f32[2,2,2,8,96,128]{5,4,3,2,1,0:T(8,128)}, u32[]{:S(2)}) copy-start(f32[2,2,2,8,96,128]{5,4,3,2,1,0:T(8,128)} %shard_map.73.fields_ref) | copy-start | bytes 9437188
where the time goes:
time: 165 us
  Pallas kernels  163 us (99%)
  local copies, waits for them, and re-layouts  1.89 us (1%)
    pallas_call x1, Pallas kernels, fused(): pl.pallas_call(migrate_kernel, out_shape=jax.ShapeDtypeStruct((2, 2, 2, B...  155 us
    pallas_call x1, Pallas kernels, fused(): pl.pallas_call(image_kernel, grid_spec=pltpu.PrefetchScalarGridSpec(num_s...  7.62 us

commit v1 on v0

--- a/solution.py
+++ b/solution.py
@@ -164,6 +164,11 @@
 ROWS = POINTS // PEERS
 LANES = 2 * ROWS
 BANDS = POINTS // LANES
+HALF = PEERS // 2
+GROUPS = 4
+INNER = 3
+OUTER = GROUPS - INNER
+SLOTS = max(INNER, OUTER)
 MESH = pl.DeviceIdType.MESH
 
 
@@ -262,37 +267,82 @@
     lane = lax.broadcasted_iota(jnp.int32, (ROWS, LANES), 1)
     low_half = lane < ROWS
 
-    def copy_f(w, d):
-        to = lax.rem(me + d, n)
+    half = me // HALF
+    pos = lax.rem(me, HALF)
+    plane = me // GROUPS
+    along = lax.rem(me, GROUPS)
+    inside = (plane == 1) | (plane == 2)
+    slots = jnp.where(inside, INNER, OUTER)
+    base = jnp.where(inside, 0, INNER)
+
+    def owner(group, i, hf):
+        return GROUPS * jnp.where(group < INNER, 1 + hf, 3 * hf) + i
+
+    def copy_f(w, group, i, hf):
+        slot = group if group < INNER else group - INNER
+        block = GROUPS * group + i
         return pltpu.make_async_remote_copy(
-            src_ref=send_f.at[w, to], dst_ref=recv_f.at[w, me],
-            send_sem=sem_fs.at[w, d], recv_sem=sem_fr.at[w, d],
-            device_id={"lat": to}, device_id_type=MESH,
+            src_ref=send_f.at[w, block], dst_ref=recv_f.at[w, slot, me],
+            send_sem=sem_fs.at[w, block, hf], recv_sem=sem_fr.at[w, slot, me],
+            device_id={"lat": owner(group, i, hf)}, device_id_type=MESH,
         )
 
-    def copy_b(w, j, d):
-        to = lax.rem(me + d, n)
-        return pltpu.make_async_remote_copy(
-            src_ref=send_b.at[w, j, to], dst_ref=recv_b.at[w, j, me],
-            send_sem=sem_bs.at[w, j, d], recv_sem=sem_br.at[w, j, d],
-            device_id={"lat": to}, device_id_type=MESH,
-        )
-
-    def got_f(w, d):
-        origin = lax.rem(me + n - d, n)
-        return pltpu.make_async_remote_copy(
-            src_ref=send_f.at[w, me], dst_ref=recv_f.at[w, origin],
-            send_sem=sem_fs.at[w, d], recv_sem=sem_fr.at[w, d],
-            device_id={"lat": origin}, device_id_type=MESH,
-        )
-
-    def got_b(w, j, d):
-        origin = lax.rem(me + n - d, n)
-        return pltpu.make_async_remote_copy(
-            src_ref=send_b.at[w, j, me], dst_ref=recv_b.at[w, j, origin],
-            send_sem=sem_bs.at[w, j, d], recv_sem=sem_br.at[w, j, d],
-            device_id={"lat": origin}, device_id_type=MESH,
-        )
+    def each_f(w, group, body):
+        @pl.loop(0, HALF)
+        def _(e):
+            i = lax.rem(e + along, GROUPS)
+            hf = lax.rem(e // GROUPS + 1 + half, 2)
+
+            @pl.when(owner(group, i, hf) != me)
+            def _():
+                body(copy_f(w, group, i, hf))
+
+    def start_f(w, group):
+        each_f(w, group, lambda copy: copy.start())
+
+        @pl.when(owner(group, along, half) == me)
+        def _():
+            slot = group if group < INNER else group - INNER
+            recv_f[w, slot, me] = send_f[w, GROUPS * group + along]
+
+    def wait_f(w, slot):
+        @pl.loop(1, PEERS)
+        def _(d):
+            origin = lax.rem(me + PEERS - d, PEERS)
+            pltpu.make_async_remote_copy(
+                src_ref=send_f.at[w, 0], dst_ref=recv_f.at[w, slot, origin],
+                send_sem=sem_fs.at[w, 0, 0], recv_sem=sem_fr.at[w, slot, origin],
+                device_id={"lat": origin}, device_id_type=MESH,
+            ).wait_recv()
+
+    def each_b(w, slot, j, body):
+        block = GROUPS * (base + slot) + along
+
+        @pl.loop(1, HALF)
+        def _(e):
+            t = lax.rem(pos + e, HALF)
+            body(pltpu.make_async_remote_copy(
+                src_ref=send_b.at[w, slot, j, t], dst_ref=recv_b.at[w, j, block],
+                send_sem=sem_bs.at[w, slot, j, t], recv_sem=sem_br.at[w, j, block],
+                device_id={"lat": HALF * half + t}, device_id_type=MESH,
+            ))
+
+    def start_b(w, slot, j):
+        each_b(w, slot, j, lambda copy: copy.start())
+        recv_b[w, j, GROUPS * (base + slot) + along] = send_b[w, slot, j, pos]
+
+    def wait_b(w, j):
+        @pl.loop(0, PEERS)
+        def _(block):
+            origin = owner(block // GROUPS, lax.rem(block, GROUPS), half)
+
+            @pl.when(origin != me)
+            def _():
+                pltpu.make_async_remote_copy(
+                    src_ref=send_b.at[w, 0, j, 0], dst_ref=recv_b.at[w, j, block],
+                    send_sem=sem_bs.at[w, 0, j, 0], recv_sem=sem_br.at[w, j, block],
+                    device_id={"lat": origin}, device_id_type=MESH,
+                ).wait_recv()
 
     def halo(w, side):
         to, take, put = (me + 1, ROWS, 0) if side == 0 else (me - 1, HMAX, HMAX + ROWS)
@@ -317,7 +367,7 @@
 
     every(greet)
 
-    def rows_forward(w):
+    def rows_forward(w, ready):
         re, im = [], []
         for q in range(RADIX):
             cut = pl.ds(q * SUB, SUB)
@@ -339,13 +389,16 @@
                     peer = RADIX * r + 2 * b
                     send_f[w, peer, c] = low
                     send_f[w, peer + 1, c] = high
-
-    def make_shift(w, j):
+            if w == 0 and r == 0:
+                ready()
+            start_f(w, r)
+
+    def make_shift(w, slot, j):
         speed = omega_ref[w] * slow_ref[j]
         vertical = speed * speed
         wide = lax.broadcasted_iota(jnp.int32, (ROWS, LANES), 1)
         tall = lax.broadcasted_iota(jnp.int32, (ROWS, LANES), 0)
-        place = ROWS * me + lax.rem(wide, ROWS)
+        place = ROWS * (GROUPS * (base + slot) + along) + lax.rem(wide, ROWS)
         ky = signed_wave(place // SUB + RADIX * lax.rem(place, SUB))
         ky2 = ky * ky
         sign = jnp.where(wide < ROWS, -1.0, 1.0)
@@ -358,14 +411,14 @@
             kx = signed_wave(r + RADIX * (lax.rem(at, SUB) + tall))
             real, imag = shift_pair(vertical - (kx * kx + ky2))
             rows = pl.ds(pl.multiple_of(ROWS * block, ROWS), ROWS)
-            shift[w, j, 0, rows, :] = real * scale
-            shift[w, j, 1, rows, :] = imag * (sign * scale)
-
-    def columns_forward(w):
+            shift[j, 0, rows, :] = real * scale
+            shift[j, 1, rows, :] = imag * (sign * scale)
+
+    def columns_forward(w, slot):
         re, im = [], []
         for q in range(RADIX):
-            re.append(recv_f[w, 4 * q : 4 * q + 4, 0].reshape(SUB, LANES))
-            im.append(recv_f[w, 4 * q : 4 * q + 4, 1].reshape(SUB, LANES))
+            re.append(recv_f[w, slot, 4 * q : 4 * q + 4, 0].reshape(SUB, LANES))
+            im.append(recv_f[w, slot, 4 * q : 4 * q + 4, 1].reshape(SUB, LANES))
         re, im = forward_four(re, im)
         for r in range(RADIX):
             pair = split(jnp.concatenate([re[r], im[r]], axis=1))
@@ -374,11 +427,11 @@
             spec[r, 0] = with_cos[:, :LANES] + with_sin[:, LANES:]
             spec[r, 1] = with_cos[:, LANES:] - with_sin[:, :LANES]
 
-    def columns_backward(w, j):
+    def columns_backward(w, slot, j):
         re, im = [], []
         for r in range(RADIX):
-            cos_shift = shift[w, j, 0, pl.ds(r * SUB, SUB), :]
-            sin_shift = shift[w, j, 1, pl.ds(r * SUB, SUB), :]
+            cos_shift = shift[j, 0, pl.ds(r * SUB, SUB), :]
+            sin_shift = shift[j, 1, pl.ds(r * SUB, SUB), :]
             new_re = spec[r, 0] * cos_shift - spec[r, 1] * sin_shift
             new_im = spec[r, 0] * sin_shift + spec[r, 1] * cos_shift
             pair = split(jnp.concatenate([new_re, new_im], axis=1))
@@ -386,10 +439,16 @@
             with_sin = table_left(tab_ref, 1, r, 1, pair)
             re.append(with_cos[:, :LANES] - with_sin[:, LANES:])
             im.append(with_cos[:, LANES:] + with_sin[:, :LANES])
-        re, im = backward_four(re, im)
-        for q in range(RADIX):
-            send_b[w, j, 4 * q : 4 * q + 4, 0] = re[q].reshape(4, ROWS, LANES)
-            send_b[w, j, 4 * q : 4 * q + 4, 1] = im[q].reshape(4, ROWS, LANES)
+        flip = (1 - 2 * half).astype(jnp.float32)
+        first = [a + b + flip * (c + d) for a, b, c, d in (
+            (re[0], re[2], re[1], re[3]), (im[0], im[2], im[1], im[3]))]
+        second = [
+            re[0] - re[2] - flip * (im[1] - im[3]),
+            im[0] - im[2] + flip * (re[1] - re[3]),
+        ]
+        for c in range(2):
+            send_b[w, slot, j, 0:4, c] = first[c].reshape(4, ROWS, LANES)
+            send_b[w, slot, j, 4:8, c] = second[c].reshape(4, ROWS, LANES)
 
     def rows_backward(w, j):
         re, im = [], []
@@ -433,25 +492,24 @@
         for w in range(2):
             out_ref[w, :, :, :, pl.ds(HMAX + ROWS, HMAX), :] = jnp.zeros((2, 2, BANDS, HMAX, LANES), jnp.float32)
 
-    rows_forward(0)
-    pl.semaphore_wait(barrier, n - 1)
-    every(lambda d: copy_f(0, d).start())
-    rows_forward(1)
-    every(lambda d: copy_f(1, d).start())
-    for w in range(2):
-        recv_f[w, me] = send_f[w, me]
+    rows_forward(0, lambda: pl.semaphore_wait(barrier, n - 1))
+    rows_forward(1, None)
+
+    @pl.loop(0, 2 * slots)
+    def _(chunk):
+        w = jnp.where(chunk < slots, 0, 1)
+        slot = chunk - slots * w
         for j in range(2):
-            make_shift(w, j)
-    for w in range(2):
-        every(lambda d: got_f(w, d).wait_recv())
-        columns_forward(w)
+            make_shift(w, slot, j)
+        wait_f(w, slot)
+        columns_forward(w, slot)
         for j in range(2):
-            columns_backward(w, j)
-            every(lambda d: copy_b(w, j, d).start())
-            recv_b[w, j, me] = send_b[w, j, me]
+            columns_backward(w, slot, j)
+            start_b(w, slot, j)
+
     for w in range(2):
         for j in range(2):
-            every(lambda d: got_b(w, j, d).wait_recv())
+            wait_b(w, j)
             rows_backward(w, j)
 
         @pl.when(me < n - 1)
@@ -463,9 +521,13 @@
             halo(w, 1).start()
 
     for w in range(2):
-        every(lambda d: copy_f(w, d).wait_send())
-        for j in range(2):
-            every(lambda d: copy_b(w, j, d).wait_send())
+        for group in range(GROUPS):
+            each_f(w, group, lambda copy: copy.wait_send())
+
+        @pl.loop(0, slots)
+        def _(slot):
+            for j in range(2):
+                each_b(w, slot, j, lambda copy: copy.wait_send())
 
         @pl.when(me < n - 1)
         def _():
@@ -505,14 +567,14 @@
         out_specs=vmem,
         scratch_shapes=[
             pltpu.VMEM((2,) + block, f32),
-            pltpu.VMEM((2,) + block, f32),
-            pltpu.VMEM((2, 2) + block, f32),
+            pltpu.VMEM((2, SLOTS) + block, f32),
+            pltpu.VMEM((2, SLOTS, 2, HALF) + block[1:], f32),
             pltpu.VMEM((2, 2) + block, f32),
             pltpu.VMEM((RADIX, 2, SUB, LANES), f32),
-            pltpu.VMEM((2, 2, 2, POINTS, LANES), f32),
+            pltpu.VMEM((2, 2, POINTS, LANES), f32),
             pltpu.VMEM((2, 2, ROWS, POINTS), f32),
-            dma((2, PEERS)), dma((2, PEERS)),
-            dma((2, 2, PEERS)), dma((2, 2, PEERS)),
+            dma((2, PEERS, 2)), dma((2, SLOTS, PEERS)),
+            dma((2, SLOTS, 2, HALF)), dma((2, 2, PEERS)),
             dma((2, 2)), dma((2, 2)),
         ],
         compiler_params=pltpu.CompilerParams(

time: 165 us -> 147 us (0.89)
  Pallas kernels: 163 us -> 144 us
    pallas_call x1, Pallas kernels: 155 us -> 136 us  [fused(): pl.pallas_call(migrate_kernel, out_shape=jax.ShapeDtypeStruct((2, 2, 2, B...]
where the time goes in v1:
time: 147 us; the launch traced here: 146 us
  Pallas kernels  144 us (98%)
  local copies, waits for them, and re-layouts  1.89 us (1%)
    pallas_call x1, Pallas kernels, fused(): pl.pallas_call(migrate_kernel, out_shape=jax.ShapeDtypeStruct((2, 2, 2, B...  136 us
    pallas_call x1, Pallas kernels, fused(): pl.pallas_call(image_kernel, grid_spec=pltpu.PrefetchScalarGridSpec(num_s...  7.74 us

profile of v1, /device:TPU:12, one launch (start us, length us, event | category | flops | bytes accessed | tf_op | source)
XLA Modules:
  0.0 145.9 jit_solution(6794340502693097202)
XLA Ops:
  0.0 0.0 copy-start.1
  0.0 136.3 %shard_map.73.fields_ref = f32[2,2,2,8,96,128]{5,4,3,2,1,0:T(8,128)} custom-call(f32[2]{0:T(128)} %omega_ref.1, f32[2]{0:T(128)} %slow_ref.1, f32[2,2,64,1024]{3,2,1,0:T(8,128)} %src_ref.1, f32[2,2,64,1024]{3,2,1,0:T(8,128)} %rec_ref.1, s32[64,1024]{1,0:T(8,128)} %index_ref.1, bf16[2,4,2,2,256,256]{5,4,3,2,1,0:T(8,128)(2,1)} %constant.2.clone.tab_ref), custom_call_target="tpu_custom_call" | custom-call | tf_op jit(solution)/shard_map/pallas_call | solution.py:563
  136.3 0.0 copy-done.1
  136.3 0.0 copy-start
  136.3 1.9 %copy-done = f32[2,2,2,8,96,128]{5,4,3,2,1,0:T(8,128)S(1)} copy-done((f32[2,2,2,8,96,128]{5,4,3,2,1,0:T(8,128)S(1)}, f32[2,2,2,8,96,128]{5,4,3,2,1,0:T(8,128)}, u32[]{:S(2)}) %copy-start) | copy-done | bytes 3145752
  138.2 7.7 %shard_map.74 = f32[16,64,1024]{2,1,0:T(8,128)} custom-call(s32[16]{0:T(128)S(1)} %copy-done.1, f32[2,2,2,8,96,128]{5,4,3,2,1,0:T(8,128)S(1)} %copy-done), custom_call_target="tpu_custom_call" | custom-call | tf_op jit(solution)/shard_map/pallas_call | solution.py:585
Async XLA Ops:
  0.0 136.3 %copy-start.1 = (s32[16]{0:T(128)S(1)}, s32[16]{0:T(128)}, u32[]{:S(2)}) copy-start(s32[16]{0:T(128)} %lags_ref.1) | copy-start | bytes 196
  136.3 1.9 %copy-start = (f32[2,2,2,8,96,128]{5,4,3,2,1,0:T(8,128)S(1)}, f32[2,2,2,8,96,128]{5,4,3,2,1,0:T(8,128)}, u32[]{:S(2)}) copy-start(f32[2,2,2,8,96,128]{5,4,3,2,1,0:T(8,128)} %shard_map.73.fields_ref) | copy-start | bytes 9437188

commit v2 on v1

--- a/solution.py
+++ b/solution.py
@@ -578,7 +578,7 @@
             dma((2, 2)), dma((2, 2)),
         ],
         compiler_params=pltpu.CompilerParams(
-            collective_id=0, has_side_effects=True, vmem_limit_bytes=56 * 2**20
+            collective_id=0, has_side_effects=True, vmem_limit_bytes=40 * 2**20
         ),
     )(omega, ref_slowness, source_field, receiver_field, interp_index, tables)
     count = lags.shape[0]
@@ -591,7 +591,7 @@
             out_specs=pl.BlockSpec((1, ROWS, POINTS), lambda i, lags: (i, 0, 0)),
         ),
         out_shape=jax.ShapeDtypeStruct((count, ROWS, POINTS), f32),
-        compiler_params=pltpu.CompilerParams(vmem_limit_bytes=32 * 2**20),
+        compiler_params=pltpu.CompilerParams(vmem_limit_bytes=24 * 2**20),
     )(lags, migrated)
 
 

time: 147 us -> 148 us (level)
  local copies, waits for them, and re-layouts: 1.89 us -> 6.9 us
  Pallas kernels: 144 us -> 140 us
    unnamed x4 -> x14, local copies, waits for them, and re-layouts: 1.89 us -> 6.9 us
    pallas_call x1, Pallas kernels: 136 us -> 132 us  [fused(): pl.pallas_call(migrate_kernel, out_shape=jax.ShapeDtypeStruct((2, 2, 2, B...]
where the time goes in v2:
time: 148 us; the launch traced here: 147 us
  Pallas kernels  140 us (95%)
  local copies, waits for them, and re-layouts  6.9 us (5%)
    pallas_call x1, Pallas kernels, fused(): pl.pallas_call(migrate_kernel, out_shape=jax.ShapeDtypeStruct((2, 2, 2, B...  132 us
    pallas_call x1, Pallas kernels, fused(): pl.pallas_call(image_kernel, grid_spec=pltpu.PrefetchScalarGridSpec(num_s...  7.71 us
    unnamed x14, local copies, waits for them, and re-layouts  6.9 us

profile of v2, /device:TPU:12, one launch (start us, length us, event | category | flops | bytes accessed | tf_op | source)
XLA Modules:
  0.0 146.9 jit_solution(6769190442206488270)
XLA Ops:
  0.0 0.0 copy-start
  0.0 2.2 %copy-done = bf16[2,4,2,2,256,256]{5,4,3,2,1,0:T(8,128)(2,1)S(1)} copy-done((bf16[2,4,2,2,256,256]{5,4,3,2,1,0:T(8,128)(2,1)S(1)}, bf16[2,4,2,2,256,256]{5,4,3,2,1,0:T(8,128)(2,1)}, u32[]{:S(2)}) %copy-start) | copy-done | bytes 4194328
  2.2 0.0 copy-start.1
  2.2 1.2 copy-done.1
  3.4 0.0 copy-start.2
  3.4 1.2 copy-done.2
  4.6 0.0 copy-start.3
  4.6 0.9 copy-done.3
  5.6 0.0 copy-start.4
  5.6 0.7 copy-done.4
  6.2 0.0 copy-start.5
  6.2 0.7 copy-done.5
  6.9 0.0 copy-start.6
  6.9 132.2 %shard_map.73.fields_ref = f32[2,2,2,8,96,128]{5,4,3,2,1,0:T(8,128)S(1)} custom-call(f32[2]{0:T(128)S(1)} %copy-done.4, f32[2]{0:T(128)S(1)} %copy-done.5, f32[2,2,64,1024]{3,2,1,0:T(8,128)S(1)} %copy-done.1, f32[2,2,64,1024]{3,2,1,0:T(8,128)S(1)} %copy-done.2, s32[64,1024]{1,0:T(8,128)S(1)} %copy-done.3, bf16[2,4,2,2,256,256]{5,4,3,2,1,0:T(8,128)(2,1)S(1)} %copy-done), custom_call_target="tpu_custom_call" | custom-call | tf_op jit(solution)/shard_map/pallas_call | solution.py:563
  139.1 0.0 copy-done.6
  139.2 7.7 %shard_map.74 = f32[16,64,1024]{2,1,0:T(8,128)} custom-call(s32[16]{0:T(128)S(1)} %copy-done.6, f32[2,2,2,8,96,128]{5,4,3,2,1,0:T(8,128)S(1)} %shard_map.73.fields_ref), custom_call_target="tpu_custom_call" | custom-call | tf_op jit(solution)/shard_map/pallas_call | solution.py:585
Async XLA Ops:
  0.0 2.2 %copy-start = (bf16[2,4,2,2,256,256]{5,4,3,2,1,0:T(8,128)(2,1)S(1)}, bf16[2,4,2,2,256,256]{5,4,3,2,1,0:T(8,128)(2,1)}, u32[]{:S(2)}) copy-start(bf16[2,4,2,2,256,256]{5,4,3,2,1,0:T(8,128)(2,1)} %constant.2.clone.tab_ref) | copy-start | bytes 12582916
  2.2 1.2 copy-start.1
  3.4 1.2 copy-start.2
  4.6 0.9 copy-start.3
  5.6 0.7 copy-start.4
  6.2 0.7 copy-start.5
  6.9 132.2 %copy-start.6 = (s32[16]{0:T(128)S(1)}, s32[16]{0:T(128)}, u32[]{:S(2)}) copy-start(s32[16]{0:T(128)} %lags_ref.1) | copy-start | bytes 196
